TPU v7x, 32 devices: a whole 2x2x4 slice. The times are simulated.
32 devices in a mesh: los: 4 (over y, x), sky: 8 (over z, core).
Axes of the slice: x: 2, y: 2, z: 4, core: 2. Of those that a mesh axis runs over, the one named last changes fastest.
Arguments:
- state: float32 [12, 32768], P(None, ('los', 'sky')), may hold values from -6 to 6
- deflection: bfloat16 [4, 2, 64, 2048], P('los', None, None, 'sky'), may hold values from -6 to 6
- shear: bfloat16 [4, 2, 96, 2048], P('los', None, None, 'sky'), may hold values from -3 to 3
- routes: int32 [4, 2, 32768, 1], P(None, None, ('los', 'sky')), may hold values from 0 to 7; in each aligned block of 1024 rows (0 to 1023, 1024 to 2047, ..., all dimensions but the last counted through in order) at most 256 rows name the same one
- patches: int32 [4, 2, 32768], P(None, None, ('los', 'sky')), may hold values from 0 to 255
Outputs:
- traced: float32 [12, 32768], P(None, ('los', 'sky'))
Inputs may be any that keep to these rules, and one draw needn't show every extreme that they name: `routes`: in each hop and plane, one device's 1024 slots name one tile at most 256 times, and exactly 256 times in some.
All inputs are finite; a program needn't handle non-finite values.
Results may differ from a plain program's by a relative error of at most 0.0003.
Values sent between devices are 32-bit elements; how exact they have to be, the bound alone decides.
A program may use at most 64 MiB of HBM per device.

v0:
```python
import functools
import math

import jax
import jax.numpy as jnp
import ml_dtypes
import numpy as np
from jax import lax
from jax.experimental import pallas as pl
from jax.experimental.pallas import tpu as pltpu
from jax.sharding import PartitionSpec as P

MESH = pl.DeviceIdType.MESH
NX, NY, COMPS = 4, 8, 5
CELLS = NX * NY
BASIS = 9
SENT = 48
WIDE = BASIS * 8


def reduction():
    i, j = np.arange(NX), np.arange(NY)
    along_x = np.stack([np.ones(NX), np.cos(2 * math.pi * i / NX), np.sin(2 * math.pi * i / NX)])
    along_y = np.stack([np.ones(NY), np.cos(2 * math.pi * j / NY), np.sin(2 * math.pi * j / NY)])
    cells = np.einsum("ai,bj->abij", along_x, along_y).reshape(BASIS, CELLS) / CELLS
    cells[np.abs(cells) < 1e-12] = 0.0
    whole = np.zeros((SENT, COMPS * CELLS))
    for ab in range(BASIS):
        for k in range(COMPS):
            whole[ab * COMPS + k, k * CELLS:(k + 1) * CELLS] = cells[ab]
    pieces, rest = [], whole
    for _ in range(3):
        piece = rest.astype(ml_dtypes.bfloat16)
        pieces.append(piece)
        rest = rest - piece.astype(np.float64)
    return np.concatenate(pieces)


def cos_turns(turns):
    folded = turns - jnp.floor(turns + 0.5)
    z = (0.25 - jnp.abs(folded)) * (2.0 * math.pi)
    q = z * z
    series = jnp.full_like(q, -1.0 / 39916800.0)
    for term in (1.0 / 362880.0, -1.0 / 5040.0, 1.0 / 120.0, -1.0 / 6.0, 1.0):
        series = series * q + term
    return series * z


def advance(pos, vel, table):
    x, y = pos[0:1] * (1.0 / NX), pos[1:2] * (1.0 / NY)
    wave = cos_turns(jnp.concatenate([x, x - 0.25, y, y - 0.25], axis=0))
    cx, sx, cy, sy = [wave[k:k + 1] for k in range(4)]
    part = [table[ab * 8:(ab + 1) * 8] for ab in range(BASIS)]
    lines = [part[3 * a] + cy * part[3 * a + 1] + sy * part[3 * a + 2] for a in range(3)]
    vals = lines[0] + cx * lines[1] + sx * lines[2]
    p11, p12, p22 = vals[2:3], vals[3:4], vals[4:5]
    top, low = pos[2:4], pos[4:6]
    turn = jnp.concatenate([vals[0:2], p11 * top + p12 * low, p12 * top + p22 * low], axis=0)
    vel = vel - turn
    return pos + 0.5 * vel, vel


def kernel(
    n_los, tiles, hops,
    state_ref, defl_ref, shear_ref, routes_ref, patches_ref, reduce_ref, out_ref,
    gathered, tables, looked, outgoing, landed,
    send_sem, recv_sem, pass_sem, move_sem, land_sem,
):
    los, sky = lax.axis_index("los"), lax.axis_index("sky")
    rays, cells = state_ref.shape[1], defl_ref.shape[3]
    pair = sky + 1 - 2 * lax.rem(sky, 2)
    peers = [lax.rem(sky + 2 * step, tiles) for step in range(1, tiles // 2)]
    after, before = lax.rem(los + 1, n_los), lax.rem(los + n_los - 1, n_los)

    barrier = pltpu.get_barrier_semaphore()
    friends = [(los, peer) for peer in peers] + [(los, pair), (after, sky), (before, sky)]
    for friend in friends:
        pl.semaphore_signal(barrier, inc=1, device_id=friend, device_id_type=MESH)

    cut = defl_ref.shape[2]
    for plane in range(2):
        found = jnp.dot(reduce_ref[:, :cut], defl_ref[0, plane], preferred_element_type=jnp.float32)
        found += jnp.dot(reduce_ref[:, cut:], shear_ref[0, plane], preferred_element_type=jnp.float32)
        gathered[plane, sky] = found[:SENT] + (found[SENT:2 * SENT] + found[2 * SENT:])
    pl.semaphore_wait(barrier, len(friends))

    def sending(plane, tile, to, sent):
        return pltpu.make_async_remote_copy(
            src_ref=gathered.at[plane, tile], dst_ref=gathered.at[plane, tile],
            send_sem=sent, recv_sem=recv_sem.at[plane, tile],
            device_id=(los, to), device_id_type=MESH,
        )

    started = []
    for plane in range(2):
        for step, to in enumerate(peers + [pair]):
            copy = sending(plane, sky, to, send_sem.at[plane, step])
            copy.start()
            started.append(copy)

    def build(plane, tile):
        wide = jnp.concatenate(
            [gathered[plane, tile, ab * COMPS:ab * COMPS + 8, :] for ab in range(BASIS)], axis=0
        )
        high = wide.astype(jnp.bfloat16).astype(jnp.float32)
        tables[plane, tile] = jnp.concatenate([high, wide - high], axis=0).astype(jnp.bfloat16)

    def arrive(plane):
        build(plane, sky)
        for step, peer in enumerate(peers):
            sending(plane, peer, pair, pass_sem.at[plane, step]).wait_recv()
            copy = sending(plane, peer, pair, pass_sem.at[plane, step])
            copy.start()
            started.append(copy)
            build(plane, peer)
        for other in [pair] + [lax.rem(pair + 2 * step, tiles) for step in range(1, tiles // 2)]:
            sending(plane, other, pair, pass_sem.at[plane, 0]).wait_recv()
            build(plane, other)

    group = min(tiles, 8)

    def lookup(hop, plane):
        patch = patches_ref[hop, plane:plane + 1, :]
        route = jnp.broadcast_to(routes_ref[hop, plane:plane + 1, :], (8, rays))
        place = lax.broadcasted_iota(jnp.int32, (cells, rays), 0)
        onehot = jnp.where(place == patch, 1.0, 0.0).astype(jnp.bfloat16)
        chosen = None
        for first in range(0, tiles, group):
            rows = tables[plane, first:first + group].reshape(group * 2 * WIDE, cells)
            raw = jnp.dot(rows, onehot, preferred_element_type=jnp.float32)
            raw = raw.reshape(group, 2, BASIS, 8, rays)
            for tile in range(group):
                both = raw[tile, 0] + raw[tile, 1]
                named = jnp.broadcast_to(route[None], both.shape) == first + tile
                chosen = both if chosen is None else jnp.where(named, both, chosen)
        looked[lax.rem(hop, 2) if not isinstance(hop, int) else hop % 2, plane] = chosen.reshape(WIDE, rays)

    state = state_ref[...]
    pos = jnp.concatenate([state[0:2], state[4:8]], axis=0)
    vel = jnp.concatenate([state[2:4], state[8:12]], axis=0)
    moves = []
    for hop in range(hops):
        for plane in range(2):
            if hop == 0:
                arrive(plane)
                lookup(hop, plane)
            pos, vel = advance(pos, vel, looked[hop % 2, plane])
        outgoing[hop, 0:2] = pos[0:2]
        outgoing[hop, 2:4] = vel[0:2]
        outgoing[hop, 4:8] = pos[2:6]
        outgoing[hop, 8:12] = vel[2:6]
        move = pltpu.make_async_remote_copy(
            src_ref=outgoing.at[hop], dst_ref=landed.at[hop],
            send_sem=move_sem.at[hop], recv_sem=land_sem.at[hop],
            device_id=(after, sky), device_id_type=MESH,
        )
        move.start()
        moves.append(move)
        if hop + 1 < hops:
            lookup(hop + 1, 0)
            lookup(hop + 1, 1)
        move.wait_recv()
        if hop + 1 < hops:
            state = landed[hop]
            pos = jnp.concatenate([state[0:2], state[4:8]], axis=0)
            vel = jnp.concatenate([state[2:4], state[8:12]], axis=0)
    out_ref[...] = landed[hops - 1]
    for copy in started + moves:
        copy.wait_send()


def body(n_los, tiles, state, deflection, shear, routes, patches):
    hops, rays, cells = routes.shape[0], state.shape[1], deflection.shape[3]
    routes = routes.reshape(patches.shape)
    vmem = pl.BlockSpec(memory_space=pltpu.VMEM)
    return pl.pallas_call(
        functools.partial(kernel, n_los, tiles, hops),
        out_shape=jax.ShapeDtypeStruct(state.shape, jnp.float32),
        in_specs=[vmem] * 6,
        out_specs=vmem,
        scratch_shapes=[
            pltpu.VMEM((2, tiles, SENT, cells), jnp.float32),
            pltpu.VMEM((2, tiles, 2 * WIDE, cells), jnp.bfloat16),
            pltpu.VMEM((2, 2, WIDE, rays), jnp.float32),
            pltpu.VMEM((hops,) + state.shape, jnp.float32),
            pltpu.VMEM((hops,) + state.shape, jnp.float32),
            pltpu.SemaphoreType.DMA((2, tiles // 2)),
            pltpu.SemaphoreType.DMA((2, tiles)),
            pltpu.SemaphoreType.DMA((2, tiles // 2)),
            pltpu.SemaphoreType.DMA((hops,)),
            pltpu.SemaphoreType.DMA((hops,)),
        ],
        compiler_params=pltpu.CompilerParams(
            collective_id=0, has_side_effects=True, vmem_limit_bytes=48 * 2**20
        ),
    )(state, deflection, shear, routes, patches, jnp.asarray(reduction()))


def solution(mesh):
    placed = (
        P(None, ("los", "sky")),
        P("los", None, None, "sky"),
        P("los", None, None, "sky"),
        P(None, None, ("los", "sky"), None),
        P(None, None, ("los", "sky")),
    )
    return jax.shard_map(
        functools.partial(body, mesh.shape["los"], mesh.shape["sky"]),
        mesh=mesh, in_specs=placed, out_specs=P(None, ("los", "sky")), check_vma=False,
    )
```

profile of v0, /device:TPU:0, one launch (start us, length us, event | category | flops | bytes accessed | tf_op | source)
XLA Modules:
  0.0 36.5 jit_solution(11475370159775137659)
XLA Ops:
  0.0 0.0 copy-start.2
  0.0 0.8 %copy.9 = s32[4,2,1024,1]{2,1,3,0:T(2,128)S(1)} copy(s32[4,2,1024,1]{2,3,1,0:T(1,128)} %param.9) | data formatting | bytes 65536
  0.8 0.0 copy-done.2
  0.8 0.0 copy-start
  0.8 0.9 %copy-done = bf16[1,2,96,256]{3,2,1,0:T(8,128)(2,1)S(1)} copy-done((bf16[1,2,96,256]{3,2,1,0:T(8,128)(2,1)S(1)}, bf16[1,2,96,256]{3,2,1,0:T(8,128)(2,1)}, u32[]{:S(2)}) %copy-start) | copy-done | bytes 98328
  1.7 0.0 copy-start.1
  1.7 0.9 %copy-done.1 = bf16[144,160]{1,0:T(8,128)(2,1)S(1)} copy-done((bf16[144,160]{1,0:T(8,128)(2,1)S(1)}, bf16[144,160]{1,0:T(8,128)(2,1)}, u32[]{:S(2)}) %copy-start.1) | copy-done | bytes 46104
  2.6 0.0 copy-start.3
  2.6 0.8 %copy-done.3 = bf16[1,2,64,256]{3,2,1,0:T(8,128)(2,1)S(1)} copy-done((bf16[1,2,64,256]{3,2,1,0:T(8,128)(2,1)S(1)}, bf16[1,2,64,256]{3,2,1,0:T(8,128)(2,1)}, u32[]{:S(2)}) %copy-start.3) | copy-done | bytes 65560
  3.5 0.0 copy-start.4
  3.5 0.8 %copy-done.4 = s32[4,2,1024]{2,1,0:T(2,128)S(1)} copy-done((s32[4,2,1024]{2,1,0:T(2,128)S(1)}, s32[4,2,1024]{2,1,0:T(2,128)}, u32[]{:S(2)}) %copy-start.4) | copy-done | bytes 32792
  4.2 31.6 %shard_map.64 = f32[12,1024]{1,0:T(8,128)S(1)} custom-call(f32[12,1024]{1,0:T(8,128)S(1)} %copy-done.2, bf16[1,2,64,256]{3,2,1,0:T(8,128)(2,1)S(1)} %copy-done.3, bf16[1,2,96,256]{3,2,1,0:T(8,128)(2,1)S(1)} %copy-done, s32[4,2,1024]{2,1,0:T(2,128)S(1)} %bitcast.3, s32[4,2,1024]{2,1,0:T(2,128)S(1)} %copy-done.4, bf16[144,160]{1,0:T(8,128)(2,1)S(1)} %copy-done.1), custom_call_target="tpu_custom_call" | custom-call | tf_op jit(solution)/shard_map/pallas_call | solution.py:176
  35.8 0.6 %copy.11 = f32[12,1024]{1,0:T(8,128)} copy(f32[12,1024]{1,0:T(8,128)S(1)} %shard_map.64) | data formatting | bytes 98304
Async XLA Ops:
  0.0 0.8 %copy-start.2 = (f32[12,1024]{1,0:T(8,128)S(1)}, f32[12,1024]{1,0:T(8,128)}, u32[]{:S(2)}) copy-start(f32[12,1024]{1,0:T(8,128)} %state_ref.1) | copy-start | bytes 147460
  0.8 0.9 %copy-start = (bf16[1,2,96,256]{3,2,1,0:T(8,128)(2,1)S(1)}, bf16[1,2,96,256]{3,2,1,0:T(8,128)(2,1)}, u32[]{:S(2)}) copy-start(bf16[1,2,96,256]{3,2,1,0:T(8,128)(2,1)} %shear_ref.1) | copy-start | bytes 294916
  1.7 0.9 %copy-start.1 = (bf16[144,160]{1,0:T(8,128)(2,1)S(1)}, bf16[144,160]{1,0:T(8,128)(2,1)}, u32[]{:S(2)}) copy-start(bf16[144,160]{1,0:T(8,128)(2,1)} %constant.2.clone.reduce_ref) | copy-start | bytes 138244
  2.6 0.8 %copy-start.3 = (bf16[1,2,64,256]{3,2,1,0:T(8,128)(2,1)S(1)}, bf16[1,2,64,256]{3,2,1,0:T(8,128)(2,1)}, u32[]{:S(2)}) copy-start(bf16[1,2,64,256]{3,2,1,0:T(8,128)(2,1)} %defl_ref.1) | copy-start | bytes 196612
  3.5 0.8 %copy-start.4 = (s32[4,2,1024]{2,1,0:T(2,128)S(1)}, s32[4,2,1024]{2,1,0:T(2,128)}, u32[]{:S(2)}) copy-start(s32[4,2,1024]{2,1,0:T(2,128)} %patches_ref.1) | copy-start | bytes 98308
where the time goes:
time: 36.8 us; the launch traced here: 36.5 us
  Pallas kernels  31.6 us (86%)
  local copies, waits for them, and re-layouts  4.84 us (13%)
    pallas_call x1, Pallas kernels, body(): pl.pallas_call(functools.partial(kernel, n_los, tiles, hops), out_shape=j...  31.6 us
    unnamed x12, local copies, waits for them, and re-layouts  4.84 us

commit v1 on v0

v1 whole, which is shorter than its diff:
```python
import functools
import math

import jax
import jax.numpy as jnp
import numpy as np
from jax import lax
from jax.experimental import pallas as pl
from jax.experimental.pallas import tpu as pltpu
from jax.sharding import PartitionSpec as P

MESH = pl.DeviceIdType.MESH
NX, NY, COMPS = 4, 8, 5
CELLS = NX * NY
BASIS = 9
SENT = BASIS * 5
HELD = 48


def reduction():
    i, j = np.arange(NX), np.arange(NY)
    along_x = np.stack([np.ones(NX), np.cos(2 * math.pi * i / NX), np.sin(2 * math.pi * i / NX)])
    along_y = np.stack([np.ones(NY), np.cos(2 * math.pi * j / NY), np.sin(2 * math.pi * j / NY)])
    cells = np.einsum("ai,bj->abij", along_x, along_y).reshape(BASIS, CELLS) / CELLS
    cells[np.abs(cells) < 1e-12] = 0.0
    whole = np.zeros((HELD, COMPS * CELLS), np.float32)
    for ab in range(BASIS):
        for k in range(COMPS):
            whole[ab * COMPS + k, k * CELLS:(k + 1) * CELLS] = cells[ab]
    return whole


def pieces(values, count):
    parts = []
    for _ in range(count):
        part = values.astype(jnp.bfloat16).astype(jnp.float32)
        parts.append(part)
        values = values - part
    return jnp.concatenate(parts, axis=0).astype(jnp.bfloat16)


def cos_turns(turns):
    folded = turns - jnp.floor(turns + 0.5)
    z = (0.25 - jnp.abs(folded)) * (2.0 * math.pi)
    q = z * z
    series = jnp.full_like(q, -1.0 / 39916800.0)
    for term in (1.0 / 362880.0, -1.0 / 5040.0, 1.0 / 120.0, -1.0 / 6.0, 1.0):
        series = series * q + term
    return series * z


def advance(pos, vel, part):
    x, y = pos[0:1] * (1.0 / NX), pos[1:2] * (1.0 / NY)
    wave = cos_turns(jnp.concatenate([x, x - 0.25, y, y - 0.25], axis=0))
    cx, sx, cy, sy = [wave[k:k + 1] for k in range(4)]
    lines = [part[3 * a] + cy * part[3 * a + 1] + sy * part[3 * a + 2] for a in range(3)]
    vals = lines[0] + cx * lines[1] + sx * lines[2]
    p11, p12, p22 = vals[2:3], vals[3:4], vals[4:5]
    top, low = pos[2:4], pos[4:6]
    turn = jnp.concatenate([vals[0:2], p11 * top + p12 * low, p12 * top + p22 * low], axis=0)
    vel = vel - turn
    return pos + 0.5 * vel, vel


def kernel(
    n_los, tiles, hops, halves,
    state_hbm, defl_hbm, shear_hbm, routes_hbm, patches_hbm, reduce_hbm, out_ref,
    state_ref, defl_ref, shear_ref, routes_ref, patches_ref, reduce_ref,
    gathered, tables, looked, outgoing, landed,
    load_sem, send_sem, recv_sem, pass_sem, move_sem, land_sem,
):
    los, sky = lax.axis_index("los"), lax.axis_index("sky")
    rays, cells = state_ref.shape[1], defl_ref.shape[3]
    part_rays = rays // halves
    pair = sky + 1 - 2 * lax.rem(sky, 2)
    peers = [lax.rem(sky + 2 * step, tiles) for step in range(1, tiles // 2)]
    mates = [pair] + [lax.rem(pair + 2 * step, tiles) for step in range(1, tiles // 2)]
    after, before = lax.rem(los + 1, n_los), lax.rem(los + n_los - 1, n_los)

    barrier = pltpu.get_barrier_semaphore()
    friends = [(los, peer) for peer in peers] + [(los, pair), (after, sky), (before, sky)]
    for friend in friends:
        pl.semaphore_signal(barrier, inc=1, device_id=friend, device_id_type=MESH)

    pairs = [
        (reduce_hbm, reduce_ref), (defl_hbm, defl_ref), (shear_hbm, shear_ref),
        (patches_hbm, patches_ref), (routes_hbm, routes_ref), (state_hbm, state_ref),
    ]
    loads = [pltpu.make_async_copy(src, dst, load_sem.at[k]) for k, (src, dst) in enumerate(pairs)]
    for load in loads:
        load.start()
    for load in loads[:3]:
        load.wait()

    def sending(plane, tile, to, sent):
        return pltpu.make_async_remote_copy(
            src_ref=gathered.at[plane, tile], dst_ref=gathered.at[plane, tile],
            send_sem=sent, recv_sem=recv_sem.at[plane, tile],
            device_id=(los, to), device_id_type=MESH,
        )

    started = []
    cut = defl_ref.shape[2]
    lower = pieces(reduce_ref[...], 3)
    for plane in range(2):
        found = jnp.dot(lower[:, :cut], defl_ref[0, plane], preferred_element_type=jnp.float32)
        found += jnp.dot(lower[:, cut:], shear_ref[0, plane], preferred_element_type=jnp.float32)
        found = found[:HELD] + (found[HELD:2 * HELD] + found[2 * HELD:])
        gathered[plane, sky] = found[:SENT]
        if plane == 0:
            pl.semaphore_wait(barrier, len(friends))
        for step, to in enumerate([pair] + peers):
            copy = sending(plane, sky, to, send_sem.at[plane, step])
            copy.start()
            started.append(copy)
    for load in loads[3:]:
        load.wait()

    def build(plane, tile):
        held = jnp.concatenate([gathered[plane, tile], jnp.zeros((HELD - SENT, cells), jnp.float32)], axis=0)
        tables[plane, tile] = pieces(held, 2)

    def from_peers(plane):
        for step, peer in enumerate(peers):
            sending(plane, peer, pair, pass_sem.at[plane, step]).wait_recv()
            copy = sending(plane, peer, pair, pass_sem.at[plane, step])
            copy.start()
            started.append(copy)
        build(plane, sky)
        for peer in peers:
            build(plane, peer)

    def from_pair(plane):
        for mate in mates:
            sending(plane, mate, pair, pass_sem.at[plane, 0]).wait_recv()
            build(plane, mate)

    group = min(tiles, 8)

    def lookup(hop, plane):
        patch = patches_ref[hop, plane:plane + 1, :]
        route = jnp.broadcast_to(routes_ref[2 * hop + plane], (8, rays))
        place = lax.broadcasted_iota(jnp.int32, (cells, rays), 0)
        onehot = jnp.where(place == patch, 1.0, 0.0).astype(jnp.bfloat16)
        chosen = None
        for first in range(0, tiles, group):
            rows = tables[plane, first:first + group].reshape(group * 2 * HELD, cells)
            raw = jnp.dot(rows, onehot, preferred_element_type=jnp.float32)
            raw = raw.reshape(group, 2, HELD // 8, 8, rays)
            for tile in range(group):
                both = raw[tile, 0] + raw[tile, 1]
                named = jnp.broadcast_to(route[None], both.shape) == first + tile
                chosen = both if chosen is None else jnp.where(named, both, chosen)
        looked[hop, plane] = chosen.reshape(HELD, rays)

    def moved(hop, half):
        return pltpu.make_async_remote_copy(
            src_ref=outgoing.at[hop, half], dst_ref=landed.at[hop, half],
            send_sem=move_sem.at[hop, half], recv_sem=land_sem.at[hop, half],
            device_id=(after, sky), device_id_type=MESH,
        )

    def step_plane(hop, plane, half, pos, vel):
        lanes = slice(half * part_rays, (half + 1) * part_rays)
        part = [looked[hop, plane, ab * COMPS:ab * COMPS + 8, lanes] for ab in range(BASIS)]
        return advance(pos, vel, part)

    def parted(state):
        return (
            jnp.concatenate([state[0:2], state[4:8]], axis=0),
            jnp.concatenate([state[2:4], state[8:12]], axis=0),
        )

    def send_on(hop, half, pos, vel):
        outgoing[hop, half, 0:2] = pos[0:2]
        outgoing[hop, half, 2:4] = vel[0:2]
        outgoing[hop, half, 4:8] = pos[2:6]
        outgoing[hop, half, 8:12] = vel[2:6]
        move = moved(hop, half)
        move.start()
        started.append(move)

    from_peers(0)
    from_pair(0)
    lookup(0, 0)
    middle = []
    for half in range(halves):
        pos, vel = parted(state_ref[:, half * part_rays:(half + 1) * part_rays])
        middle.append(step_plane(0, 0, half, pos, vel))
    if hops > 1:
        lookup(1, 0)
    from_peers(1)
    if hops > 2:
        lookup(2, 0)
    from_pair(1)
    lookup(0, 1)
    for half in range(halves):
        send_on(0, half, *step_plane(0, 1, half, *middle[half]))
    for hop in range(1, hops):
        lookup(hop, 1)
        if hop + 2 < hops:
            lookup(hop + 2, 0)
        for half in range(halves):
            moved(hop - 1, half).wait_recv()
            pos, vel = parted(landed[hop - 1, half])
            for plane in range(2):
                pos, vel = step_plane(hop, plane, half, pos, vel)
            send_on(hop, half, pos, vel)
    for half in range(halves):
        moved(hops - 1, half).wait_recv()
        out_ref[:, half * part_rays:(half + 1) * part_rays] = landed[hops - 1, half]
    for copy in started:
        copy.wait_send()


def body(n_los, tiles, state, deflection, shear, routes, patches):
    hops, rays, cells = routes.shape[0], state.shape[1], deflection.shape[3]
    halves = 2
    routes = routes.reshape(hops * 2, 1, rays)
    inputs = (state, deflection, shear, routes, patches, jnp.asarray(reduction()))
    return pl.pallas_call(
        functools.partial(kernel, n_los, tiles, hops, halves),
        out_shape=jax.ShapeDtypeStruct(state.shape, jnp.float32),
        in_specs=[pl.BlockSpec(memory_space=pltpu.HBM)] * 6,
        out_specs=pl.BlockSpec(memory_space=pltpu.VMEM),
        scratch_shapes=[pltpu.VMEM(array.shape, array.dtype) for array in inputs] + [
            pltpu.VMEM((2, tiles, SENT, cells), jnp.float32),
            pltpu.VMEM((2, tiles, 2 * HELD, cells), jnp.bfloat16),
            pltpu.VMEM((hops, 2, HELD, rays), jnp.float32),
            pltpu.VMEM((hops, halves, state.shape[0], rays // halves), jnp.float32),
            pltpu.VMEM((hops, halves, state.shape[0], rays // halves), jnp.float32),
            pltpu.SemaphoreType.DMA((len(inputs),)),
            pltpu.SemaphoreType.DMA((2, tiles // 2)),
            pltpu.SemaphoreType.DMA((2, tiles)),
            pltpu.SemaphoreType.DMA((2, tiles // 2)),
            pltpu.SemaphoreType.DMA((hops, halves)),
            pltpu.SemaphoreType.DMA((hops, halves)),
        ],
        compiler_params=pltpu.CompilerParams(
            collective_id=0, has_side_effects=True, vmem_limit_bytes=64 * 2**20
        ),
    )(*inputs)


def solution(mesh):
    placed = (
        P(None, ("los", "sky")),
        P("los", None, None, "sky"),
        P("los", None, None, "sky"),
        P(None, None, ("los", "sky"), None),
        P(None, None, ("los", "sky")),
    )
    return jax.shard_map(
        functools.partial(body, mesh.shape["los"], mesh.shape["sky"]),
        mesh=mesh, in_specs=placed, out_specs=P(None, ("los", "sky")), check_vma=False,
    )
```

time: 36.8 us -> 33 us (0.90)
  local copies, waits for them, and re-layouts: 4.84 us -> 1.47 us
    unnamed x12 -> x1, local copies, waits for them, and re-layouts: 4.84 us -> 1.47 us
where the time goes in v1:
time: 33 us; the launch traced here: 32.8 us
  Pallas kernels  31.3 us (95%)
  local copies, waits for them, and re-layouts  1.47 us (4%)
    pallas_call x1, Pallas kernels, body(): pl.pallas_call(functools.partial(kernel, n_los, tiles, hops, halves), out...  31.3 us
    unnamed x1, local copies, waits for them, and re-layouts  1.47 us

profile of v1, /device:TPU:0, one launch (start us, length us, event | category | flops | bytes accessed | tf_op | source)
XLA Modules:
  0.0 32.8 jit_solution(15037599332169062561)
XLA Ops:
  0.0 31.3 %shard_map.64 = f32[12,1024]{1,0:T(8,128)} custom-call(f32[12,1024]{1,0:T(8,128)} %state_hbm.1, bf16[1,2,64,256]{3,2,1,0:T(8,128)(2,1)} %defl_hbm.1, bf16[1,2,96,256]{3,2,1,0:T(8,128)(2,1)} %shear_hbm.1, s32[8,1,1024]{2,1,0:T(1,128)} %bitcast.1, s32[4,2,1024]{2,1,0:T(2,128)} %patches_hbm.1, f32[48,160]{1,0:T(8,128)} %constant.2.clone.reduce_hbm), custom_call_target="tpu_custom_call" | custom-call | tf_op jit(solution)/shard_map/pallas_call | solution.py:221
  31.3 1.5 %copy.8 = f32[12,1024]{1,0:T(8,128)} copy(f32[12,1024]{1,0:T(8,128)} %shard_map.64) | data formatting | bytes 98304

commit v2 on v1

--- a/solution.py
+++ b/solution.py
@@ -36,7 +36,7 @@
         part = values.astype(jnp.bfloat16).astype(jnp.float32)
         parts.append(part)
         values = values - part
-    return jnp.concatenate(parts, axis=0).astype(jnp.bfloat16)
+    return [part.astype(jnp.bfloat16) for part in parts]
 
 
 def cos_turns(turns):
@@ -64,10 +64,10 @@
 
 def kernel(
     n_los, tiles, hops, halves,
-    state_hbm, defl_hbm, shear_hbm, routes_hbm, patches_hbm, reduce_hbm, out_ref,
+    state_hbm, defl_hbm, shear_hbm, routes_hbm, patches_hbm, reduce_hbm, out_hbm,
     state_ref, defl_ref, shear_ref, routes_ref, patches_ref, reduce_ref,
     gathered, tables, looked, outgoing, landed,
-    load_sem, send_sem, recv_sem, pass_sem, move_sem, land_sem,
+    load_sem, send_sem, recv_sem, pass_sem, move_sem, land_sem, store_sem,
 ):
     los, sky = lax.axis_index("los"), lax.axis_index("sky")
     rays, cells = state_ref.shape[1], defl_ref.shape[3]
@@ -101,7 +101,7 @@
 
     started = []
     cut = defl_ref.shape[2]
-    lower = pieces(reduce_ref[...], 3)
+    lower = jnp.concatenate(pieces(reduce_ref[...], 3), axis=0)
     for plane in range(2):
         found = jnp.dot(lower[:, :cut], defl_ref[0, plane], preferred_element_type=jnp.float32)
         found += jnp.dot(lower[:, cut:], shear_ref[0, plane], preferred_element_type=jnp.float32)
@@ -110,15 +110,23 @@
         if plane == 0:
             pl.semaphore_wait(barrier, len(friends))
         for step, to in enumerate([pair] + peers):
+            if plane == 1:
+                started[step].wait_send()
             copy = sending(plane, sky, to, send_sem.at[plane, step])
             copy.start()
             started.append(copy)
+    started = started[tiles // 2:]
     for load in loads[3:]:
         load.wait()
 
-    def build(plane, tile):
+    half_tiles = tiles // 2
+    own = lax.rem(sky, 2)
+
+    def build(plane, tile, other):
         held = jnp.concatenate([gathered[plane, tile], jnp.zeros((HELD - SENT, cells), jnp.float32)], axis=0)
-        tables[plane, tile] = pieces(held, 2)
+        high, low = pieces(held, 2)
+        tables[plane, other, tile // 2, :, :cells] = high
+        tables[plane, other, tile // 2, :, cells:] = low
 
     def from_peers(plane):
         for step, peer in enumerate(peers):
@@ -126,31 +134,33 @@
             copy = sending(plane, peer, pair, pass_sem.at[plane, step])
             copy.start()
             started.append(copy)
-        build(plane, sky)
+        build(plane, sky, 0)
         for peer in peers:
-            build(plane, peer)
+            build(plane, peer, 0)
 
     def from_pair(plane):
         for mate in mates:
             sending(plane, mate, pair, pass_sem.at[plane, 0]).wait_recv()
-            build(plane, mate)
-
-    group = min(tiles, 8)
-
-    def lookup(hop, plane):
+            build(plane, mate, 1)
+
+    group = min(half_tiles, 8)
+
+    def lookup(hop, plane, others=(0, 1)):
         patch = patches_ref[hop, plane:plane + 1, :]
         route = jnp.broadcast_to(routes_ref[2 * hop + plane], (8, rays))
         place = lax.broadcasted_iota(jnp.int32, (cells, rays), 0)
         onehot = jnp.where(place == patch, 1.0, 0.0).astype(jnp.bfloat16)
-        chosen = None
-        for first in range(0, tiles, group):
-            rows = tables[plane, first:first + group].reshape(group * 2 * HELD, cells)
-            raw = jnp.dot(rows, onehot, preferred_element_type=jnp.float32)
-            raw = raw.reshape(group, 2, HELD // 8, 8, rays)
-            for tile in range(group):
-                both = raw[tile, 0] + raw[tile, 1]
-                named = jnp.broadcast_to(route[None], both.shape) == first + tile
-                chosen = both if chosen is None else jnp.where(named, both, chosen)
+        onehot = jnp.concatenate([onehot, onehot], axis=0)
+        chosen = None if others[0] == 0 else looked[hop, plane].reshape(HELD // 8, 8, rays)
+        for other in others:
+            core = own if other == 0 else 1 - own
+            for first in range(0, half_tiles, group):
+                rows = tables[plane, other, first:first + group].reshape(group * HELD, 2 * cells)
+                raw = jnp.dot(rows, onehot, preferred_element_type=jnp.float32)
+                raw = raw.reshape(group, HELD // 8, 8, rays)
+                for k in range(group):
+                    named = jnp.broadcast_to(route[None], raw[k].shape) == 2 * (first + k) + core
+                    chosen = raw[k] if chosen is None else jnp.where(named, raw[k], chosen)
         looked[hop, plane] = chosen.reshape(HELD, rays)
 
     def moved(hop, half):
@@ -181,8 +191,9 @@
         started.append(move)
 
     from_peers(0)
+    lookup(0, 0, (0,))
     from_pair(0)
-    lookup(0, 0)
+    lookup(0, 0, (1,))
     middle = []
     for half in range(halves):
         pos, vel = parted(state_ref[:, half * part_rays:(half + 1) * part_rays])
@@ -190,27 +201,32 @@
     if hops > 1:
         lookup(1, 0)
     from_peers(1)
-    if hops > 2:
-        lookup(2, 0)
+    lookup(0, 1, (0,))
     from_pair(1)
-    lookup(0, 1)
+    lookup(0, 1, (1,))
     for half in range(halves):
         send_on(0, half, *step_plane(0, 1, half, *middle[half]))
     for hop in range(1, hops):
         lookup(hop, 1)
-        if hop + 2 < hops:
-            lookup(hop + 2, 0)
+        if hop > 1:
+            lookup(hop, 0)
         for half in range(halves):
             moved(hop - 1, half).wait_recv()
             pos, vel = parted(landed[hop - 1, half])
             for plane in range(2):
                 pos, vel = step_plane(hop, plane, half, pos, vel)
             send_on(hop, half, pos, vel)
+    stores = []
     for half in range(halves):
         moved(hops - 1, half).wait_recv()
-        out_ref[:, half * part_rays:(half + 1) * part_rays] = landed[hops - 1, half]
+        lanes = pl.ds(half * part_rays, part_rays)
+        store = pltpu.make_async_copy(landed.at[hops - 1, half], out_hbm.at[:, lanes], store_sem.at[half])
+        store.start()
+        stores.append(store)
     for copy in started:
         copy.wait_send()
+    for store in stores:
+        store.wait()
 
 
 def body(n_los, tiles, state, deflection, shear, routes, patches):
@@ -222,10 +238,10 @@
         functools.partial(kernel, n_los, tiles, hops, halves),
         out_shape=jax.ShapeDtypeStruct(state.shape, jnp.float32),
         in_specs=[pl.BlockSpec(memory_space=pltpu.HBM)] * 6,
-        out_specs=pl.BlockSpec(memory_space=pltpu.VMEM),
+        out_specs=pl.BlockSpec(memory_space=pltpu.HBM),
         scratch_shapes=[pltpu.VMEM(array.shape, array.dtype) for array in inputs] + [
             pltpu.VMEM((2, tiles, SENT, cells), jnp.float32),
-            pltpu.VMEM((2, tiles, 2 * HELD, cells), jnp.bfloat16),
+            pltpu.VMEM((2, 2, tiles // 2, HELD, 2 * cells), jnp.bfloat16),
             pltpu.VMEM((hops, 2, HELD, rays), jnp.float32),
             pltpu.VMEM((hops, halves, state.shape[0], rays // halves), jnp.float32),
             pltpu.VMEM((hops, halves, state.shape[0], rays // halves), jnp.float32),
@@ -235,6 +251,7 @@
             pltpu.SemaphoreType.DMA((2, tiles // 2)),
             pltpu.SemaphoreType.DMA((hops, halves)),
             pltpu.SemaphoreType.DMA((hops, halves)),
+            pltpu.SemaphoreType.DMA((halves,)),
         ],
         compiler_params=pltpu.CompilerParams(
             collective_id=0, has_side_effects=True, vmem_limit_bytes=64 * 2**20

time: 33 us -> 32.4 us (0.982)
  Pallas kernels: 31.3 us -> 30.8 us
    pallas_call x1, Pallas kernels: 31.3 us -> 30.8 us  [body(): pl.pallas_call(functools.partial(kernel, n_los, tiles, hops, halves), out...]
where the time goes in v2:
time: 32.4 us; the launch traced here: 32.3 us
  Pallas kernels  30.8 us (95%)
  local copies, waits for them, and re-layouts  1.47 us (5%)
    pallas_call x1, Pallas kernels, body(): pl.pallas_call(functools.partial(kernel, n_los, tiles, hops, halves), out...  30.8 us
    unnamed x1, local copies, waits for them, and re-layouts  1.47 us

profile of v2, /device:TPU:0, one launch (start us, length us, event | category | flops | bytes accessed | tf_op | source)
XLA Modules:
  0.0 32.3 jit_solution(604834826085586889)
XLA Ops:
  0.0 30.8 %shard_map.64 = f32[12,1024]{1,0:T(8,128)} custom-call(f32[12,1024]{1,0:T(8,128)} %state_hbm.1, bf16[1,2,64,256]{3,2,1,0:T(8,128)(2,1)} %defl_hbm.1, bf16[1,2,96,256]{3,2,1,0:T(8,128)(2,1)} %shear_hbm.1, s32[8,1,1024]{2,1,0:T(1,128)} %bitcast.1, s32[4,2,1024]{2,1,0:T(2,128)} %patches_hbm.1, f32[48,160]{1,0:T(8,128)} %constant.2.clone.reduce_hbm), custom_call_target="tpu_custom_call" | custom-call | tf_op jit(solution)/shard_map/pallas_call | solution.py:237
  30.8 1.5 %copy.8 = f32[12,1024]{1,0:T(8,128)} copy(f32[12,1024]{1,0:T(8,128)} %shard_map.64) | data formatting | bytes 98304

commit v3 on v2

--- a/solution.py
+++ b/solution.py
@@ -66,8 +66,8 @@
     n_los, tiles, hops, halves,
     state_hbm, defl_hbm, shear_hbm, routes_hbm, patches_hbm, reduce_hbm, out_hbm,
     state_ref, defl_ref, shear_ref, routes_ref, patches_ref, reduce_ref,
-    gathered, tables, looked, outgoing, landed,
-    load_sem, send_sem, recv_sem, pass_sem, move_sem, land_sem, store_sem,
+    gathered, tables, looked, lent, outgoing, landed,
+    load_sem, send_sem, recv_sem, pass_sem, move_sem, land_sem, lend_sem, lent_sem, store_sem,
 ):
     los, sky = lax.axis_index("los"), lax.axis_index("sky")
     rays, cells = state_ref.shape[1], defl_ref.shape[3]
@@ -78,7 +78,10 @@
     after, before = lax.rem(los + 1, n_los), lax.rem(los + n_los - 1, n_los)
 
     barrier = pltpu.get_barrier_semaphore()
-    friends = [(los, peer) for peer in peers] + [(los, pair), (after, sky), (before, sky)]
+    home = lax.rem(los + 2, n_los)
+    friends = [(los, peer) for peer in peers] + [(los, pair), (after, sky), (before, sky), (home, sky)]
+    if n_los != 4:
+        friends.append((lax.rem(los + n_los - 2, n_los), sky))
     for friend in friends:
         pl.semaphore_signal(barrier, inc=1, device_id=friend, device_id_type=MESH)
 
@@ -167,12 +170,26 @@
         return pltpu.make_async_remote_copy(
             src_ref=outgoing.at[hop, half], dst_ref=landed.at[hop, half],
             send_sem=move_sem.at[hop, half], recv_sem=land_sem.at[hop, half],
+            device_id=(after if hop < hops - 2 else home, sky), device_id_type=MESH,
+        )
+
+    def lending(plane):
+        return pltpu.make_async_remote_copy(
+            src_ref=looked.at[hops - 1, plane], dst_ref=lent.at[plane],
+            send_sem=lend_sem.at[plane], recv_sem=lent_sem.at[plane],
             device_id=(after, sky), device_id_type=MESH,
         )
+
+    def lend(plane):
+        lookup(hops - 1, plane)
+        copy = lending(plane)
+        copy.start()
+        started.append(copy)
 
     def step_plane(hop, plane, half, pos, vel):
         lanes = slice(half * part_rays, (half + 1) * part_rays)
-        part = [looked[hop, plane, ab * COMPS:ab * COMPS + 8, lanes] for ab in range(BASIS)]
+        table = looked.at[hop, plane] if hop < hops - 1 else lent.at[plane]
+        part = [table[ab * COMPS:ab * COMPS + 8, lanes] for ab in range(BASIS)]
         return advance(pos, vel, part)
 
     def parted(state):
@@ -186,6 +203,12 @@
         outgoing[hop, half, 2:4] = vel[0:2]
         outgoing[hop, half, 4:8] = pos[2:6]
         outgoing[hop, half, 8:12] = vel[2:6]
+        if hop == hops - 1:
+            lanes = pl.ds(half * part_rays, part_rays)
+            store = pltpu.make_async_copy(outgoing.at[hop, half], out_hbm.at[:, lanes], store_sem.at[half])
+            store.start()
+            stores.append(store)
+            return
         move = moved(hop, half)
         move.start()
         started.append(move)
@@ -194,35 +217,30 @@
     lookup(0, 0, (0,))
     from_pair(0)
     lookup(0, 0, (1,))
-    middle = []
+    middle, stores = [], []
     for half in range(halves):
         pos, vel = parted(state_ref[:, half * part_rays:(half + 1) * part_rays])
         middle.append(step_plane(0, 0, half, pos, vel))
-    if hops > 1:
-        lookup(1, 0)
+    lend(0)
     from_peers(1)
     lookup(0, 1, (0,))
     from_pair(1)
     lookup(0, 1, (1,))
     for half in range(halves):
         send_on(0, half, *step_plane(0, 1, half, *middle[half]))
+    lend(1)
     for hop in range(1, hops):
-        lookup(hop, 1)
-        if hop > 1:
-            lookup(hop, 0)
+        for plane in range(2):
+            if hop < hops - 1:
+                lookup(hop, plane)
+            else:
+                lending(plane).wait_recv()
         for half in range(halves):
             moved(hop - 1, half).wait_recv()
             pos, vel = parted(landed[hop - 1, half])
             for plane in range(2):
                 pos, vel = step_plane(hop, plane, half, pos, vel)
             send_on(hop, half, pos, vel)
-    stores = []
-    for half in range(halves):
-        moved(hops - 1, half).wait_recv()
-        lanes = pl.ds(half * part_rays, part_rays)
-        store = pltpu.make_async_copy(landed.at[hops - 1, half], out_hbm.at[:, lanes], store_sem.at[half])
-        store.start()
-        stores.append(store)
     for copy in started:
         copy.wait_send()
     for store in stores:
@@ -243,14 +261,17 @@
             pltpu.VMEM((2, tiles, SENT, cells), jnp.float32),
             pltpu.VMEM((2, 2, tiles // 2, HELD, 2 * cells), jnp.bfloat16),
             pltpu.VMEM((hops, 2, HELD, rays), jnp.float32),
+            pltpu.VMEM((2, HELD, rays), jnp.float32),
             pltpu.VMEM((hops, halves, state.shape[0], rays // halves), jnp.float32),
-            pltpu.VMEM((hops, halves, state.shape[0], rays // halves), jnp.float32),
+            pltpu.VMEM((hops - 1, halves, state.shape[0], rays // halves), jnp.float32),
             pltpu.SemaphoreType.DMA((len(inputs),)),
             pltpu.SemaphoreType.DMA((2, tiles // 2)),
             pltpu.SemaphoreType.DMA((2, tiles)),
             pltpu.SemaphoreType.DMA((2, tiles // 2)),
-            pltpu.SemaphoreType.DMA((hops, halves)),
-            pltpu.SemaphoreType.DMA((hops, halves)),
+            pltpu.SemaphoreType.DMA((hops - 1, halves)),
+            pltpu.SemaphoreType.DMA((hops - 1, halves)),
+            pltpu.SemaphoreType.DMA((2,)),
+            pltpu.SemaphoreType.DMA((2,)),
             pltpu.SemaphoreType.DMA((halves,)),
         ],
         compiler_params=pltpu.CompilerParams(

time: 32.4 us -> 33.5 us (1.034)
  Pallas kernels: 30.8 us -> 31.8 us
    pallas_call x1, Pallas kernels: 30.8 us -> 31.8 us  [body(): pl.pallas_call(functools.partial(kernel, n_los, tiles, hops, halves), out...]
where the time goes in v3:
time: 33.5 us; the launch traced here: 33.3 us
  Pallas kernels  31.8 us (95%)
  local copies, waits for them, and re-layouts  1.47 us (4%)
    pallas_call x1, Pallas kernels, body(): pl.pallas_call(functools.partial(kernel, n_los, tiles, hops, halves), out...  31.8 us
    unnamed x1, local copies, waits for them, and re-layouts  1.47 us

profile of v3, /device:TPU:0, one launch (start us, length us, event | category | flops | bytes accessed | tf_op | source)
XLA Modules:
  0.0 33.3 jit_solution(4797719737505822285)
XLA Ops:
  0.0 31.8 %shard_map.64 = f32[12,1024]{1,0:T(8,128)} custom-call(f32[12,1024]{1,0:T(8,128)} %state_hbm.1, bf16[1,2,64,256]{3,2,1,0:T(8,128)(2,1)} %defl_hbm.1, bf16[1,2,96,256]{3,2,1,0:T(8,128)(2,1)} %shear_hbm.1, s32[8,1,1024]{2,1,0:T(1,128)} %bitcast.1, s32[4,2,1024]{2,1,0:T(2,128)} %patches_hbm.1, f32[48,160]{1,0:T(8,128)} %constant.2.clone.reduce_hbm), custom_call_target="tpu_custom_call" | custom-call | tf_op jit(solution)/shard_map/pallas_call | solution.py:255
  31.8 1.5 %copy.8 = f32[12,1024]{1,0:T(8,128)} copy(f32[12,1024]{1,0:T(8,128)} %shard_map.64) | data formatting | bytes 98304

commit v4 on v2

--- a/solution.py
+++ b/solution.py
@@ -131,9 +131,7 @@
     def from_peers(plane):
         for step, peer in enumerate(peers):
             sending(plane, peer, pair, pass_sem.at[plane, step]).wait_recv()
-            copy = sending(plane, peer, pair, pass_sem.at[plane, step])
-            copy.start()
-            started.append(copy)
+            sending(plane, peer, pair, pass_sem.at[plane, step]).start()
         build(plane, sky, 0)
         for peer in peers:
             build(plane, peer, 0)
@@ -145,23 +143,33 @@
 
     group = min(half_tiles, 8)
 
+    block = min(rays, 512)
+
     def lookup(hop, plane, others=(0, 1)):
-        patch = patches_ref[hop, plane:plane + 1, :]
-        route = jnp.broadcast_to(routes_ref[2 * hop + plane], (8, rays))
-        place = lax.broadcasted_iota(jnp.int32, (cells, rays), 0)
-        onehot = jnp.where(place == patch, 1.0, 0.0).astype(jnp.bfloat16)
-        onehot = jnp.concatenate([onehot, onehot], axis=0)
-        chosen = None if others[0] == 0 else looked[hop, plane].reshape(HELD // 8, 8, rays)
-        for other in others:
-            core = own if other == 0 else 1 - own
-            for first in range(0, half_tiles, group):
-                rows = tables[plane, other, first:first + group].reshape(group * HELD, 2 * cells)
-                raw = jnp.dot(rows, onehot, preferred_element_type=jnp.float32)
-                raw = raw.reshape(group, HELD // 8, 8, rays)
-                for k in range(group):
-                    named = jnp.broadcast_to(route[None], raw[k].shape) == 2 * (first + k) + core
-                    chosen = raw[k] if chosen is None else jnp.where(named, raw[k], chosen)
-        looked[hop, plane] = chosen.reshape(HELD, rays)
+        def lookup_block(index, carry):
+            lanes = pl.ds(pl.multiple_of(index * block, block), block)
+            both = patches_ref[hop, :, lanes]
+            patch = jnp.where(plane == 0, both[0:1], both[1:2])
+            route = jnp.broadcast_to(routes_ref[2 * hop + plane, :, lanes], (8, block))
+            place = lax.broadcasted_iota(jnp.int32, (cells, block), 0)
+            onehot = jnp.where(place == patch, 1.0, 0.0).astype(jnp.bfloat16)
+            onehot = jnp.concatenate([onehot, onehot], axis=0)
+            chosen = None
+            if others[0] != 0:
+                chosen = looked[hop, plane, :, lanes].reshape(HELD // 8, 8, block)
+            for other in others:
+                core = own if other == 0 else 1 - own
+                for first in range(0, half_tiles, group):
+                    rows = tables[plane, other, first:first + group].reshape(group * HELD, 2 * cells)
+                    raw = jnp.dot(rows, onehot, preferred_element_type=jnp.float32)
+                    raw = raw.reshape(group, HELD // 8, 8, block)
+                    for k in range(group):
+                        named = jnp.broadcast_to(route[None], raw[k].shape) == 2 * (first + k) + core
+                        chosen = raw[k] if chosen is None else jnp.where(named, raw[k], chosen)
+            looked[hop, plane, :, lanes] = chosen.reshape(HELD, block)
+            return carry
+
+        lax.fori_loop(0, rays // block, lookup_block, 0)
 
     def moved(hop, half):
         return pltpu.make_async_remote_copy(
@@ -186,36 +194,37 @@
         outgoing[hop, half, 2:4] = vel[0:2]
         outgoing[hop, half, 4:8] = pos[2:6]
         outgoing[hop, half, 8:12] = vel[2:6]
-        move = moved(hop, half)
-        move.start()
-        started.append(move)
-
-    from_peers(0)
-    lookup(0, 0, (0,))
-    from_pair(0)
-    lookup(0, 0, (1,))
-    middle = []
+        moved(hop, half).start()
+
+    def first_hop(plane, rays_now):
+        from_peers(plane)
+        lookup(0, plane, (0,))
+        from_pair(plane)
+        lookup(0, plane, (1,))
+        return tuple(step_plane(0, plane, half, *rays_now[half]) for half in range(halves))
+
+    at_start = tuple(
+        parted(state_ref[:, half * part_rays:(half + 1) * part_rays]) for half in range(halves)
+    )
+    after_first = lax.fori_loop(0, 2, first_hop, at_start)
     for half in range(halves):
-        pos, vel = parted(state_ref[:, half * part_rays:(half + 1) * part_rays])
-        middle.append(step_plane(0, 0, half, pos, vel))
-    if hops > 1:
-        lookup(1, 0)
-    from_peers(1)
-    lookup(0, 1, (0,))
-    from_pair(1)
-    lookup(0, 1, (1,))
-    for half in range(halves):
-        send_on(0, half, *step_plane(0, 1, half, *middle[half]))
-    for hop in range(1, hops):
-        lookup(hop, 1)
-        if hop > 1:
-            lookup(hop, 0)
+        send_on(0, half, *after_first[half])
+
+    def later_hop(hop, carry):
+        def both_planes(plane, inner):
+            lookup(hop, plane)
+            return inner
+
+        lax.fori_loop(0, 2, both_planes, 0)
         for half in range(halves):
             moved(hop - 1, half).wait_recv()
-            pos, vel = parted(landed[hop - 1, half])
+            rays_now = parted(landed[hop - 1, half])
             for plane in range(2):
-                pos, vel = step_plane(hop, plane, half, pos, vel)
-            send_on(hop, half, pos, vel)
+                rays_now = step_plane(hop, plane, half, *rays_now)
+            send_on(hop, half, *rays_now)
+        return carry
+
+    lax.fori_loop(1, hops, later_hop, 0)
     stores = []
     for half in range(halves):
         moved(hops - 1, half).wait_recv()
@@ -225,6 +234,12 @@
         stores.append(store)
     for copy in started:
         copy.wait_send()
+    for plane in range(2):
+        for step, peer in enumerate(peers):
+            sending(plane, peer, pair, pass_sem.at[plane, step]).wait_send()
+    for hop in range(hops):
+        for half in range(halves):
+            moved(hop, half).wait_send()
     for store in stores:
         store.wait()
 

time: 32.4 us -> 33 us (1.019)
  Pallas kernels: 30.8 us -> 31.3 us
    pallas_call x1, Pallas kernels: 30.8 us -> 31.3 us  [body(): pl.pallas_call(functools.partial(kernel, n_los, tiles, hops, halves), out...]
where the time goes in v4:
time: 33 us; the launch traced here: 32.8 us
  Pallas kernels  31.3 us (95%)
  local copies, waits for them, and re-layouts  1.47 us (4%)
    pallas_call x1, Pallas kernels, body(): pl.pallas_call(functools.partial(kernel, n_los, tiles, hops, halves), out...  31.3 us
    unnamed x1, local copies, waits for them, and re-layouts  1.47 us

profile of v4, /device:TPU:0, one launch (start us, length us, event | category | flops | bytes accessed | tf_op | source)
XLA Modules:
  0.0 32.8 jit_solution(7986427555008142684)
XLA Ops:
  0.0 31.3 %shard_map.64 = f32[12,1024]{1,0:T(8,128)} custom-call(f32[12,1024]{1,0:T(8,128)} %state_hbm.1, bf16[1,2,64,256]{3,2,1,0:T(8,128)(2,1)} %defl_hbm.1, bf16[1,2,96,256]{3,2,1,0:T(8,128)(2,1)} %shear_hbm.1, s32[8,1,1024]{2,1,0:T(1,128)} %bitcast.1, s32[4,2,1024]{2,1,0:T(2,128)} %patches_hbm.1, f32[48,160]{1,0:T(8,128)} %constant.2.clone.reduce_hbm), custom_call_target="tpu_custom_call" | custom-call | tf_op jit(solution)/shard_map/pallas_call | solution.py:252
  31.3 1.5 %copy.8 = f32[12,1024]{1,0:T(8,128)} copy(f32[12,1024]{1,0:T(8,128)} %shard_map.64) | data formatting | bytes 98304

commit v5 on v4

--- a/solution.py
+++ b/solution.py
@@ -143,33 +143,29 @@
 
     group = min(half_tiles, 8)
 
-    block = min(rays, 512)
+    block = rays
 
     def lookup(hop, plane, others=(0, 1)):
-        def lookup_block(index, carry):
-            lanes = pl.ds(pl.multiple_of(index * block, block), block)
-            both = patches_ref[hop, :, lanes]
-            patch = jnp.where(plane == 0, both[0:1], both[1:2])
-            route = jnp.broadcast_to(routes_ref[2 * hop + plane, :, lanes], (8, block))
-            place = lax.broadcasted_iota(jnp.int32, (cells, block), 0)
-            onehot = jnp.where(place == patch, 1.0, 0.0).astype(jnp.bfloat16)
-            onehot = jnp.concatenate([onehot, onehot], axis=0)
-            chosen = None
-            if others[0] != 0:
-                chosen = looked[hop, plane, :, lanes].reshape(HELD // 8, 8, block)
-            for other in others:
-                core = own if other == 0 else 1 - own
-                for first in range(0, half_tiles, group):
-                    rows = tables[plane, other, first:first + group].reshape(group * HELD, 2 * cells)
-                    raw = jnp.dot(rows, onehot, preferred_element_type=jnp.float32)
-                    raw = raw.reshape(group, HELD // 8, 8, block)
-                    for k in range(group):
-                        named = jnp.broadcast_to(route[None], raw[k].shape) == 2 * (first + k) + core
-                        chosen = raw[k] if chosen is None else jnp.where(named, raw[k], chosen)
-            looked[hop, plane, :, lanes] = chosen.reshape(HELD, block)
-            return carry
-
-        lax.fori_loop(0, rays // block, lookup_block, 0)
+        lanes = slice(None)
+        both = patches_ref[hop, :, lanes]
+        patch = jnp.where(plane == 0, both[0:1], both[1:2])
+        route = jnp.broadcast_to(routes_ref[2 * hop + plane, :, lanes], (8, block))
+        place = lax.broadcasted_iota(jnp.int32, (cells, block), 0)
+        onehot = jnp.where(place == patch, 1.0, 0.0).astype(jnp.bfloat16)
+        onehot = jnp.concatenate([onehot, onehot], axis=0)
+        chosen = None
+        if others[0] != 0:
+            chosen = looked[hop, plane, :, lanes].reshape(HELD // 8, 8, block)
+        for other in others:
+            core = own if other == 0 else 1 - own
+            for first in range(0, half_tiles, group):
+                rows = tables[plane, other, first:first + group].reshape(group * HELD, 2 * cells)
+                raw = jnp.dot(rows, onehot, preferred_element_type=jnp.float32)
+                raw = raw.reshape(group, HELD // 8, 8, block)
+                for k in range(group):
+                    named = jnp.broadcast_to(route[None], raw[k].shape) == 2 * (first + k) + core
+                    chosen = raw[k] if chosen is None else jnp.where(named, raw[k], chosen)
+        looked[hop, plane, :, lanes] = chosen.reshape(HELD, block)
 
     def moved(hop, half):
         return pltpu.make_async_remote_copy(

time: 33 us -> 32.5 us (0.985)
  Pallas kernels: 31.3 us -> 30.8 us
    pallas_call x1, Pallas kernels: 31.3 us -> 30.8 us  [body(): pl.pallas_call(functools.partial(kernel, n_los, tiles, hops, halves), out...]
where the time goes in v5:
time: 32.5 us; the launch traced here: 32.3 us
  Pallas kernels  30.8 us (95%)
  local copies, waits for them, and re-layouts  1.47 us (5%)
    pallas_call x1, Pallas kernels, body(): pl.pallas_call(functools.partial(kernel, n_los, tiles, hops, halves), out...  30.8 us
    unnamed x1, local copies, waits for them, and re-layouts  1.47 us

profile of v5, /device:TPU:0, one launch (start us, length us, event | category | flops | bytes accessed | tf_op | source)
XLA Modules:
  0.0 32.3 jit_solution(6823613755995421408)
XLA Ops:
  0.0 30.8 %shard_map.64 = f32[12,1024]{1,0:T(8,128)} custom-call(f32[12,1024]{1,0:T(8,128)} %state_hbm.1, bf16[1,2,64,256]{3,2,1,0:T(8,128)(2,1)} %defl_hbm.1, bf16[1,2,96,256]{3,2,1,0:T(8,128)(2,1)} %shear_hbm.1, s32[8,1,1024]{2,1,0:T(1,128)} %bitcast.1, s32[4,2,1024]{2,1,0:T(2,128)} %patches_hbm.1, f32[48,160]{1,0:T(8,128)} %constant.2.clone.reduce_hbm), custom_call_target="tpu_custom_call" | custom-call | tf_op jit(solution)/shard_map/pallas_call | solution.py:248
  30.8 1.5 %copy.8 = f32[12,1024]{1,0:T(8,128)} copy(f32[12,1024]{1,0:T(8,128)} %shard_map.64) | data formatting | bytes 98304
